TPU v7x, 256 devices: a whole 4x4x8 slice. The times are simulated.
256 devices in a mesh: ctx: 8 (over z), tp: 32 (over y, x, core).
Axes of the slice: x: 4, y: 4, z: 8, core: 2. Of those that a mesh axis runs over, the one named last changes fastest.
Arguments:
- tokens: bfloat16 [1024, 8192], P('ctx', 'tp'), may hold values from -6 to 6
- inner_weight: bfloat16 [8192, 8192], P(None, 'tp'), may hold values from -0.0625 to 0.0625
- gate_weight: bfloat16 [8192, 8192], P(None, 'tp'), may hold values from -0.0625 to 0.0625
- conv_weight: float32 [4, 8192], P(None, 'tp'), may hold values from -3 to 3
- conv_bias: float32 [8192], P('tp'), may hold values from -3 to 3
- proj_weight: bfloat16 [8192, 544], P('tp'), may hold values from -0.0625 to 0.0625
- step_weight: bfloat16 [512, 8192], P(None, 'tp'), may hold values from -0.25 to 0.25
- step_bias: float32 [8192], P('tp'), may hold values from -4 to -0.5
- decay_rate: float32 [8192, 16], P('tp'), may hold values from 1e-05 to 2
- skip_gain: float32 [8192], P('tp'), may hold values from -1 to 2
- out_weight: bfloat16 [8192, 8192], P('tp'), may hold values from -0.125 to 0.125
- carried_state: float32 [8192, 16], P('tp'), may hold values from -6 to 6
Outputs:
- mixed: bfloat16 [1024, 8192], P('ctx', 'tp')
- boundary_states: float32 [8, 8192, 16], P('ctx', 'tp')
All inputs are finite; a program needn't handle non-finite values.
Results may differ from a plain program's by a relative error of at most 0.025.
Values may be sent and summed in bfloat16 or wider, within the bound.
A program may use at most 64 MiB of HBM per device.

v0:
```python
import math

import jax
import jax.numpy as jnp
from jax import lax
from jax.sharding import PartitionSpec as P

STATE = 16
DT_RANK = 512


def from_behind(value, axis, by):
    peers = lax.axis_size(axis)
    pairs = [(i, i + by) for i in range(peers) if 0 <= i + by < peers]
    return lax.ppermute(value, axis, pairs)


def compose(earlier, latter):
    return (earlier[0] * latter[0], latter[0] * earlier[1] + latter[1])


def on_device(
    tokens,
    inner_weight,
    gate_weight,
    conv_weight,
    conv_bias,
    proj_weight,
    step_weight,
    step_bias,
    decay_rate,
    skip_gain,
    out_weight,
    carried_state,
):
    row_count = tokens.shape[0]
    channels = inner_weight.shape[1]
    shard_piece = lax.all_gather(tokens, "tp", axis=1, tiled=True)
    inner_acc = jnp.dot(shard_piece, inner_weight, preferred_element_type=jnp.float32)
    gate_acc = jnp.dot(shard_piece, gate_weight, preferred_element_type=jnp.float32)
    inner_x = inner_acc.astype(jnp.bfloat16)
    gate = gate_acc.astype(jnp.bfloat16)
    kernel = conv_weight.shape[0]
    tail_rows = from_behind(inner_x[row_count - (kernel - 1) :], "ctx", 1)
    leading = lax.axis_index("ctx") == 0
    padded = jnp.concatenate([tail_rows, inner_x], axis=0).astype(jnp.float32)
    summed = jnp.broadcast_to(conv_bias[None, :], (row_count, channels))
    for offset in range(kernel):
        summed = summed + conv_weight[offset][None, :] * padded[offset : offset + row_count]
    conv_x = jax.nn.silu(summed).astype(jnp.bfloat16)
    partial_proj = jnp.dot(conv_x, proj_weight, preferred_element_type=jnp.float32)
    proj = lax.psum(partial_proj.astype(jnp.bfloat16), "tp").astype(jnp.float32)
    low = proj[:, :DT_RANK].astype(jnp.bfloat16)
    step = jax.nn.softplus(
        jnp.dot(low, step_weight, preferred_element_type=jnp.float32) + step_bias[None, :]
    )
    b_in = proj[:, DT_RANK : DT_RANK + STATE]
    c_out = proj[:, DT_RANK + STATE :]
    conv_float = conv_x.astype(jnp.float32)
    decay_t = jnp.transpose(decay_rate)
    carried_t = jnp.transpose(carried_state)
    drive = step * conv_float
    block_rows = math.gcd(row_count, 128)
    block_count = row_count // block_rows

    def run_block(carry, pieces):
        step_blk, drive_blk, b_blk, c_blk = pieces
        factors = jnp.exp(-step_blk[:, None, :] * decay_t[None, :, :])
        inputs = drive_blk[:, None, :] * b_blk[:, :, None]
        cum_blk, local_blk = lax.associative_scan(compose, (factors, inputs), axis=0)
        hidden_blk = local_blk + cum_blk * carry[None]
        readout_blk = jnp.sum(hidden_blk * c_blk[:, :, None], axis=1)
        return (hidden_blk[-1], readout_blk)

    blocked = (
        step.reshape(block_count, block_rows, channels),
        drive.reshape(block_count, block_rows, channels),
        b_in.reshape(block_count, block_rows, STATE),
        c_out.reshape(block_count, block_rows, STATE),
    )
    end_state, readout_local = lax.scan(
        run_block, jnp.zeros((STATE, channels), jnp.float32), blocked
    )
    readout_local = readout_local.reshape(row_count, channels)
    step_total = jnp.cumsum(step, axis=0)
    end_decay = jnp.exp(-decay_t * step_total[-1][None, :])
    entering = jnp.where(leading, carried_t, jnp.zeros_like(carried_t))
    for turn in range(lax.axis_size("ctx") - 1):
        handed = from_behind(end_decay * entering + end_state, "ctx", 1)
        entering = jnp.where(leading, carried_t, handed)
    readout = readout_local
    for state_index in range(STATE):
        readout = (
            readout
            + c_out[:, state_index : state_index + 1]
            * jnp.exp(-decay_t[state_index][None, :] * step_total)
            * entering[state_index][None, :]
        )
    boundary = jnp.transpose(end_decay * entering + end_state)[None]
    gated = (
        (readout + skip_gain[None, :] * conv_float) * jax.nn.silu(gate.astype(jnp.float32))
    ).astype(jnp.bfloat16)
    summed_out = lax.psum_scatter(
        lax.dot_general(
            out_weight, gated, (((0,), (1,)), ((), ())), preferred_element_type=jnp.float32
        ).astype(jnp.bfloat16),
        "tp",
        scatter_dimension=0,
        tiled=True,
    ).astype(jnp.float32)
    mixed = jnp.transpose(summed_out).astype(jnp.bfloat16)
    return (mixed, boundary)


def solution(mesh):
    in_specs = (
        P("ctx", "tp"),
        P(None, "tp"),
        P(None, "tp"),
        P(None, "tp"),
        P("tp"),
        P("tp", None),
        P(None, "tp"),
        P("tp"),
        P("tp", None),
        P("tp"),
        P("tp", None),
        P("tp", None),
    )
    out_specs = (P("ctx", "tp"), P("ctx", "tp", None))
    return jax.shard_map(
        on_device, mesh=mesh, in_specs=in_specs, out_specs=out_specs, check_vma=False
    )
```

profile of v0, /device:TPU:64, one launch (start us, length us, event | category | flops | bytes accessed | tf_op | source)
XLA Modules:
  0.0 600.1 jit_solution(8134441334210557052)
XLA Ops:
  8.0 54.5 %all-gather.2.cloned.1.call-done = bf16[128,8192]{1,0:T(8,128)(2,1)} async-done(((bf16[128,256]{1,0:T(8,128)(2,1)}), bf16[128,8192]{1,0:T(8,128)(2,1)}) %all-gather.2.cloned.1.call-update) | async-done | bytes 2097168 | tf_op jit(solution)/shard_map/all_gather | solution.py:38
  62.5 3.5 convolution_convert_fusion.3
  66.1 3.5 collective-permute-start
  69.6 2.0 collective-permute-done
  72.7 107.9 %all-reduce.30.cloned.1.call-done = bf16[128,544]{0,1:T(8,128)(2,1)} async-done(((bf16[128,544]{0,1:T(8,128)(2,1)}), bf16[128,544]{0,1:T(8,128)(2,1)}) %all-reduce.30.cloned.1.call-update) | async-done | bytes 139280 | tf_op jit(solution)/shard_map/psum | solution.py:52
  180.6 1.3 fusion.167
  182.0 1.8 convert_multiply_fusion.1
  193.7 2.0 pad.116
  195.6 2.0 pad.117
  197.6 1.2 pad.131
  199.6 1.2 pad.130
  200.8 1.5 add.309
  203.2 1.5 add.297
  204.7 1.4 pad_maximum_fusion.9
  206.1 3.3 pad.132
  209.4 1.4 pad_maximum_fusion.8
  210.7 3.3 pad.118
  214.0 3.3 pad.119
  217.3 3.3 pad.133
  220.6 1.6 add.310
  222.3 1.9 fusion.95
  224.1 1.6 add.299
  226.4 4.8 pad.134
  231.2 1.6 pad_maximum_fusion.6
  232.8 4.8 pad.120
  237.6 4.8 pad.121
  242.4 4.8 pad.135
  247.3 1.8 add.311
  249.1 2.3 fusion.4
  252.9 8.7 %pad.136 = f32[32,16,256]{2,1,0:T(8,128)} pad(f32[16,16,256]{2,1,0:T(8,128)} %pad_maximum_fusion.5, f32[]{:T(128)} %constant.30.clone.1), padding=0_1_1x0_0_0x0_0_0 | pad | bytes 786436 | tf_op jit(solution)/shard_map/while/body/eval_jaxpr/pad | solution.py:70
  261.7 1.7 pad_maximum_fusion.4
  263.4 8.7 %pad.122 = f32[32,16,256]{2,1,0:T(8,128)} pad(f32[16,16,256]{2,1,0:T(8,128)} %pad_maximum_fusion.4, f32[]{:T(128)} %constant.30.clone.1), padding=0_1_1x0_0_0x0_0_0 | pad | bytes 786436 | tf_op jit(solution)/shard_map/while/body/eval_jaxpr/pad | solution.py:70
  272.1 8.7 %pad.123 = f32[32,16,256]{2,1,0:T(8,128)} pad(f32[16,16,256]{2,1,0:T(8,128)} %add.301, f32[]{:T(128)} %constant.30.clone.1), padding=1_0_1x0_0_0x0_0_0 | pad | bytes 786436 | tf_op jit(solution)/shard_map/while/body/eval_jaxpr/pad | solution.py:70
  280.7 8.7 %pad.137 = f32[32,16,256]{2,1,0:T(8,128)} pad(f32[16,16,256]{2,1,0:T(8,128)} %add.311, f32[]{:T(128)} %constant.30.clone.1), padding=1_0_1x0_0_0x0_0_0 | pad | bytes 786436 | tf_op jit(solution)/shard_map/while/body/eval_jaxpr/pad | solution.py:70
  289.5 2.1 add.312
  291.6 2.9 fusion.3
  296.3 11.6 %pad.138 = f32[64,16,256]{2,1,0:T(8,128)S(1)} pad(f32[32,16,256]{2,1,0:T(8,128)} %pad_maximum_fusion.3, f32[]{:T(128)} %constant.30.clone.1), padding=0_1_1x0_0_0x0_0_0 | pad | bytes 1572868 | tf_op jit(solution)/shard_map/while/body/eval_jaxpr/pad | solution.py:70
  307.8 1.9 pad_maximum_fusion.2
  309.7 15.6 %pad.124 = f32[64,16,256]{2,1,0:T(8,128)} pad(f32[32,16,256]{2,1,0:T(8,128)} %pad_maximum_fusion.2, f32[]{:T(128)} %constant.30.clone.1), padding=0_1_1x0_0_0x0_0_0 | pad | bytes 1572868 | tf_op jit(solution)/shard_map/while/body/eval_jaxpr/pad | solution.py:70
  325.4 15.6 %pad.125 = f32[64,16,256]{2,1,0:T(8,128)} pad(f32[32,16,256]{2,1,0:T(8,128)} %add.303, f32[]{:T(128)} %constant.30.clone.1), padding=1_0_1x0_0_0x0_0_0 | pad | bytes 1572868 | tf_op jit(solution)/shard_map/while/body/eval_jaxpr/pad | solution.py:70
  341.0 15.6 %pad.139 = f32[64,16,256]{2,1,0:T(8,128)} pad(f32[32,16,256]{2,1,0:T(8,128)} %add.312, f32[]{:T(128)} %constant.30.clone.1), padding=1_0_1x0_0_0x0_0_0 | pad | bytes 1572868 | tf_op jit(solution)/shard_map/while/body/eval_jaxpr/pad | solution.py:70
  356.7 2.5 add.313
  359.2 3.3 fusion.2
  364.9 20.6 %pad.140 = f32[128,16,256]{2,1,0:T(8,128)} pad(f32[64,16,256]{2,1,0:T(8,128)S(1)} %pad_maximum_fusion.1, f32[]{:T(128)} %constant.30.clone.1), padding=0_1_1x0_0_0x0_0_0 | pad | bytes 3145732 | tf_op jit(solution)/shard_map/while/body/eval_jaxpr/pad | solution.py:70
  385.5 20.6 %pad.126 = f32[128,16,256]{2,1,0:T(8,128)} pad(f32[64,16,256]{2,1,0:T(8,128)S(1)} %pad_maximum_fusion, f32[]{:T(128)} %constant.30.clone.1), padding=0_1_1x0_0_0x0_0_0 | pad | bytes 3145732 | tf_op jit(solution)/shard_map/while/body/eval_jaxpr/pad | solution.py:70
  406.1 20.6 %pad.127 = f32[128,16,256]{2,1,0:T(8,128)} pad(f32[64,16,256]{2,1,0:T(8,128)S(1)} %add.305, f32[]{:T(128)} %constant.30.clone.1), padding=1_0_1x0_0_0x0_0_0 | pad | bytes 3145732 | tf_op jit(solution)/shard_map/while/body/eval_jaxpr/pad | solution.py:70
  426.7 20.5 %pad.141 = f32[128,16,256]{2,1,0:T(8,128)} pad(f32[64,16,256]{2,1,0:T(8,128)S(1)} %copy-done.9, f32[]{:T(128)} %constant.30.clone.1), padding=1_0_1x0_0_0x0_0_0 | pad | bytes 3145732 | tf_op jit(solution)/shard_map/while/body/eval_jaxpr/pad | solution.py:70
  447.3 4.5 multiply_reduce_fusion
  451.8 3.5 collective-permute-start.1
  455.2 2.2 collective-permute-done.1
  457.4 3.9 collective-permute-start.2
  461.4 1.7 collective-permute-done.2
  463.1 5.1 collective-permute-start.3
  468.2 1.4 collective-permute-done.3
  469.7 5.4 collective-permute-start.4
  475.1 1.4 collective-permute-done.4
  476.5 5.4 collective-permute-start.5
  481.9 1.4 collective-permute-done.5
  483.4 5.4 collective-permute-start.6
  488.9 1.4 collective-permute-done.6
  490.2 5.4 collective-permute-start.7
  495.7 1.4 collective-permute-done.7
  497.7 7.4 %fusion = bf16[8192,128]{0,1:T(8,128)(2,1)} fusion(bf16[256,8192]{1,0:T(8,128)(2,1)} %param.22, bf16[128,256]{1,0:T(8,128)(2,1)S(1)} %multiply_convert_fusion, bf16[128,8192]{1,0:T(8,128)(2,1)S(1)} %copy-done.5, bf16[8192,256]{1,0:T(8,128)(2,1)} %param.14, f32[128,256]{1,0:T(8,128)S(1)} %copy-done.24, f32[128,256]{1,0:T(8,128)S(1)} %get-tuple-element.20, ...), kind=kOutput, calls=%fused_computation.1 | convolution fusion | flops 1077248000 | bytes 12952576 | tf_op jit(solution)/shard_map/dot_general | solution.py:104
  505.2 88.4 %reduce-scatter.2.cloned.1.call-done = bf16[256,128]{0,1:T(8,128)(2,1)} async-done(((bf16[8192,128]{0,1:T(8,128)(2,1)}), bf16[256,128]{0,1:T(8,128)(2,1)}) %reduce-scatter.2.cloned.1.call-update) | async-done | bytes 65552 | tf_op jit(solution)/shard_map/reduce_scatter | solution.py:103
  (141 shorter events, 20.4 us)
Async XLA Ops:
  7.2 64.5 %copy-start = (bf16[256,544]{0,1:T(8,128)(2,1)S(1)}, bf16[256,544]{0,1:T(8,128)(2,1)}, u32[]{:S(2)}) copy-start(bf16[256,544]{0,1:T(8,128)(2,1)} %param.17) | copy-start | bytes 835588
  7.2 55.3 %all-gather.2.cloned.1.call-start = ((), (), s32[]{:S(2)}) async-start(), calls=%async_computation.1 | async-start | bytes 2162688 | tf_op jit(solution)/shard_map/all_gather | solution.py:38
  7.9 61.6 %copy-start.37 = (f32[4,256]{1,0:T(4,128)S(1)}, f32[4,256]{1,0:T(4,128)}, u32[]{:S(2)}) copy-start(f32[4,256]{1,0:T(4,128)} %param.15) | copy-start | bytes 12292
  7.9 63.7 %copy-start.38 = (f32[256]{0:T(256)S(1)}, f32[256]{0:T(256)}, u32[]{:S(2)}) copy-start(f32[256]{0:T(256)} %param.16) | copy-start | bytes 3076
  7.9 174.1 %copy-start.27 = (bf16[512,256]{1,0:T(8,128)(2,1)S(1)}, bf16[512,256]{1,0:T(8,128)(2,1)}, u32[]{:S(2)}) copy-start(bf16[512,256]{1,0:T(8,128)(2,1)} %param.18) | copy-start | bytes 786436
  7.9 174.1 %copy-start.39 = (f32[256]{0:T(256)S(1)}, f32[256]{0:T(256)}, u32[]{:S(2)}) copy-start(f32[256]{0:T(256)} %param.19) | copy-start | bytes 3076
  8.0 172.7 %all-reduce.30.cloned.1.call-start = ((), (), s32[]{:S(2)}) async-start(), calls=%async_computation.2 | async-start | bytes 278528 | tf_op jit(solution)/shard_map/psum | solution.py:52
  66.1 117.8 %copy-start.16 = (f32[256,16]{0,1:T(8,128)S(1)}, f32[256,16]{0,1:T(8,128)}, u32[]{:S(2)}) copy-start(f32[256,16]{0,1:T(8,128)} %param.20) | copy-start | bytes 49156
  66.1 5.5 collective-permute-start
  72.6 521.0 %reduce-scatter.2.cloned.1.call-start = ((), (), s32[]{:S(2)}) async-start(), calls=%async_computation.3 | async-start | bytes 2162688 | tf_op jit(solution)/shard_map/reduce_scatter | solution.py:103
  184.5 1.8 copy-start.1
  186.3 2.9 copy-start.6
  187.8 1.4 copy-start.12
  187.8 2.1 copy-start.13
  189.1 1.3 copy-start.17
  189.2 1.3 copy-start.18
  190.5 1.3 copy-start.20
  190.5 1.3 copy-start.21
  210.7 15.0 %copy-start.35 = (f32[1,16,256]{2,1,0:T(8,128)S(1)}, f32[1,16,256]{2,1,0:T(8,128)}, u32[]{:S(2)}) copy-start(f32[1,16,256]{2,1,0:T(8,128)} %slice.629) | copy-start | bytes 49156
  210.7 20.5 %copy-start.34 = (f32[1,16,256]{2,1,0:T(8,128)S(1)}, f32[1,16,256]{2,1,0:T(8,128)}, u32[]{:S(2)}) copy-start(f32[1,16,256]{2,1,0:T(8,128)} %slice.606) | copy-start | bytes 49156
  237.6 14.6 %copy-start.33 = (f32[1,16,256]{2,1,0:T(8,128)S(1)}, f32[1,16,256]{2,1,0:T(8,128)}, u32[]{:S(2)}) copy-start(f32[1,16,256]{2,1,0:T(8,128)} %slice.628) | copy-start | bytes 49156
  247.3 4.1 copy-start.14
  247.3 4.1 copy-start.15
  249.1 12.5 %copy-start.32 = (f32[1,16,256]{2,1,0:T(8,128)S(1)}, f32[1,16,256]{2,1,0:T(8,128)}, u32[]{:S(2)}) copy-start(f32[1,16,256]{2,1,0:T(8,128)} %slice.605) | copy-start | bytes 49156
  291.6 2.9 copy-start.7
  291.6 2.9 copy-start.8
  291.6 3.8 copy-start.31
  294.5 13.3 %copy-start.30 = (f32[1,16,256]{2,1,0:T(8,128)S(1)}, f32[1,16,256]{2,1,0:T(8,128)}, u32[]{:S(2)}) copy-start(f32[1,16,256]{2,1,0:T(8,128)} %slice.604) | copy-start | bytes 49156
  356.7 2.5 copy-start.2
  356.7 2.5 copy-start.3
  356.7 2.5 copy-start.4
  362.5 0.7 copy-start.36
  362.5 1.4 copy-start.25
  362.5 2.3 copy-start.11
  362.5 2.3 copy-start.29
  364.1 0.6 copy-start.23
  364.9 20.6 %copy-start.10 = (f32[63,16,256]{2,1,0:T(8,128)S(1)}, f32[63,16,256]{2,1,0:T(8,128)}, u32[]{:S(2)}) copy-start(f32[63,16,256]{2,1,0:T(8,128)} %get-tuple-element.22) | copy-start | bytes 3096580
  364.9 20.6 %copy-start.28 = (f32[1,16,256]{2,1,0:T(8,128)S(1)}, f32[1,16,256]{2,1,0:T(8,128)}, u32[]{:S(2)}) copy-start(f32[1,16,256]{2,1,0:T(8,128)} %slice.603) | copy-start | bytes 49156
  406.1 20.6 %copy-start.9 = (f32[64,16,256]{2,1,0:T(8,128)S(1)}, f32[64,16,256]{2,1,0:T(8,128)}, u32[]{:S(2)}) copy-start(f32[64,16,256]{2,1,0:T(8,128)} %add.313) | copy-start | bytes 3145732
  426.7 20.5 %copy-start.26 = (f32[128,16]{1,0:T(8,128)S(1)}, f32[128,16]{1,0:T(8,128)}, u32[]{:S(2)}) copy-start(f32[128,16]{1,0:T(8,128)} %copy.15) | copy-start | bytes 24580
  447.2 4.5 copy-start.19
  447.2 41.6 %copy-start.22 = (bf16[128,544]{0,1:T(8,128)(2,1)S(1)}, bf16[128,544]{0,1:T(8,128)(2,1)}, u32[]{:S(2)}) copy-start(bf16[128,544]{0,1:T(8,128)(2,1)} %all-reduce.30.cloned.1.call-done) | copy-start | bytes 417796
  447.2 50.5 %copy-start.5 = (bf16[128,8192]{1,0:T(8,128)(2,1)S(1)}, bf16[128,8192]{1,0:T(8,128)(2,1)}, u32[]{:S(2)}) copy-start(bf16[128,8192]{1,0:T(8,128)(2,1)} %all-gather.2.cloned.1.call-done) | copy-start | bytes 6291460
  447.2 50.5 %copy-start.24 = (f32[128,256]{1,0:T(8,128)S(1)}, f32[128,256]{1,0:T(8,128)}, u32[]{:S(2)}) copy-start(f32[128,256]{1,0:T(8,128)} %copy-done.23) | copy-start | bytes 393220
  447.2 50.5 %copy-start.40 = (f32[256]{0:T(256)S(1)}, f32[256]{0:T(256)}, u32[]{:S(2)}) copy-start(f32[256]{0:T(256)} %param.21) | copy-start | bytes 3076
  451.8 5.6 collective-permute-start.1
  457.4 5.6 collective-permute-start.2
  463.1 6.6 %collective-permute-start.3 = (f32[16,256]{1,0:T(8,128)S(1)}, f32[16,256]{1,0:T(8,128)S(1)}, u32[]{:S(2)}, u32[]{:S(2)}) collective-permute-start(f32[16,256]{1,0:T(8,128)S(1)} %fusion.157), channel_id=1, source_target_pairs={{0,32},{32,64},{64,96},{96,128},{128,160},{160,192},{192,224},{1,3... | collective-permute-start | bytes 49160 | tf_op jit(solution)/shard_map/ppermute | solution.py:15
  469.7 6.8 %collective-permute-start.4 = (f32[16,256]{1,0:T(8,128)S(1)}, f32[16,256]{1,0:T(8,128)S(1)}, u32[]{:S(2)}, u32[]{:S(2)}) collective-permute-start(f32[16,256]{1,0:T(8,128)S(1)} %fusion.159), channel_id=1, source_target_pairs={{0,32},{32,64},{64,96},{96,128},{128,160},{160,192},{192,224},{1,3... | collective-permute-start | bytes 49160 | tf_op jit(solution)/shard_map/ppermute | solution.py:15
  476.5 6.8 %collective-permute-start.5 = (f32[16,256]{1,0:T(8,128)S(1)}, f32[16,256]{1,0:T(8,128)S(1)}, u32[]{:S(2)}, u32[]{:S(2)}) collective-permute-start(f32[16,256]{1,0:T(8,128)S(1)} %fusion.161), channel_id=1, source_target_pairs={{0,32},{32,64},{64,96},{96,128},{128,160},{160,192},{192,224},{1,3... | collective-permute-start | bytes 49160 | tf_op jit(solution)/shard_map/ppermute | solution.py:15
  483.4 6.8 %collective-permute-start.6 = (f32[16,256]{1,0:T(8,128)S(1)}, f32[16,256]{1,0:T(8,128)S(1)}, u32[]{:S(2)}, u32[]{:S(2)}) collective-permute-start(f32[16,256]{1,0:T(8,128)S(1)} %fusion.163), channel_id=1, source_target_pairs={{0,32},{32,64},{64,96},{96,128},{128,160},{160,192},{192,224},{1,3... | collective-permute-start | bytes 49160 | tf_op jit(solution)/shard_map/ppermute | solution.py:15
  490.2 6.8 %collective-permute-start.7 = (f32[16,256]{1,0:T(8,128)S(1)}, f32[16,256]{1,0:T(8,128)S(1)}, u32[]{:S(2)}, u32[]{:S(2)}) collective-permute-start(f32[16,256]{1,0:T(8,128)S(1)} %fusion.165), channel_id=1, source_target_pairs={{0,32},{32,64},{64,96},{96,128},{128,160},{160,192},{192,224},{1,3... | collective-permute-start | bytes 49160 | tf_op jit(solution)/shard_map/ppermute | solution.py:15
Sparse Core Ops, SparseCore 0:
  10.5 51.9 all-gather.1
  72.7 107.8 all-reduce.29
  505.3 88.2 reduce-scatter.1
where the time goes:
time: 611 us; the launch traced here: 600 us
  waiting for transfers between devices  264 us (43%)
  local copies, waits for them, and re-layouts  224 us (37%)
  other arithmetic  45.8 us (7%)
  starting transfers between devices  37.8 us (6%)
  between operations  14.3 us (2%)
  matrix products  13.7 us (2%)
    pad x24, local copies, waits for them, and re-layouts, run_block(): lax.associative_scan(compose, (factors, inputs), axis=0)  214 us
    psum x1, waiting for transfers between devices, on_device(): proj = lax.psum(partial_proj.astype(jnp.bfloat16), 'tp').astype(jnp.float32)  108 us
    reduce_scatter x1, waiting for transfers between devices, on_device(): lax.psum_scatter(lax.dot_general(out_weight, gated, (((0,), (1,)), ((), (...  88.4 us
    all_gather x1, waiting for transfers between devices, on_device(): shard_piece = lax.all_gather(tokens, 'tp', axis=1, tiled=True)  54.5 us
    ppermute x8, starting transfers between devices, from_behind(): return lax.ppermute(value, axis, pairs)  37.6 us
    add x12, other arithmetic, run_block(): lax.associative_scan(compose, (factors, inputs), axis=0)  15.2 us
    ppermute x8, waiting for transfers between devices, from_behind(): return lax.ppermute(value, axis, pairs)  12.9 us
    add x12, other arithmetic, compose(): return (earlier[0] * latter[0], latter[0] * earlier[1] + latter[1])  12.3 us
  transfers between devices with their start and end apart: 11, of which 11 were waited for; matrix products, arithmetic and copies ran while one was open for 0% of the time, Pallas kernels for 0%

commit v1 on v0

v1 whole, which is shorter than its diff:
```python
import functools

import jax
import jax.numpy as jnp
from jax import lax
from jax.experimental import pallas as pl
from jax.experimental.pallas import tpu as pltpu
from jax.sharding import PartitionSpec as P

STATE = 16
DT_RANK = 512
MESH = pl.DeviceIdType.MESH
BF16 = jnp.bfloat16
F32 = jnp.float32


def dot(a, b):
    return jnp.dot(a, b, preferred_element_type=F32)


def dot_t(a, b):
    return lax.dot_general(a, b, (((1,), (1,)), ((), ())), preferred_element_type=F32)


def silu(v):
    return v * jax.nn.sigmoid(v)


def plane_sides(n_tp):
    chips = n_tp // 2
    side = 1
    while side * side < chips:
        side *= 2
    return chips // side, side


def kernel(
    n_ctx, n_tp, tokens_hbm, iw_hbm, gw_hbm, cw_hbm, cb_hbm, pw_hbm, sw_hbm, sb_hbm, dr_hbm, sg_hbm, ow_hbm, cs_hbm,
    mixed, boundary,
    x_buf, iw, gw, ow, pw, sw, cw, cb, sb, sg, dr, cs, acc, gate, pad, tail_in,
    p_send, p_recv, p_more, p_res, step_ref, drive_ref, conv_ref, h_buf, b_chunk, c_chunk, state_out, state_in, q_buf, y_buf,
    part, sib_part, mine, s1_send, s1_a, s1_b, s2_send, s2_a, s2_b,
    load_sem, own_send, own_recv, sib_send, sib_recv, tail_sem, red_sem, more_sem, res_sem, state_send, state_recv,
    rs_sib_send, rs_sib_recv, s1_send_sem, s1_a_sem, s1_b_sem, s2_send_sem, s2_a_sem, s2_b_sem,
):
    ny, nx = plane_sides(n_tp)
    chips = ny * nx
    rows, width = tokens_hbm.shape
    half = rows // 2
    s, me = lax.axis_index("ctx"), lax.axis_index("tp")
    core, chip = lax.rem(me, 2), me // 2
    cx, cy = lax.rem(chip, nx), chip // nx

    def chip_at(dx, dy):
        return lax.rem(cy + dy + ny, ny) * nx + lax.rem(cx + dx + nx, nx)

    def tp_at(dx, dy, other=False):
        return chip_at(dx, dy) * 2 + ((1 - core) if other else core)

    def remote(src, dst, send, recv, to, ctx=None):
        return pltpu.make_async_remote_copy(
            src_ref=src, dst_ref=dst, send_sem=send, recv_sem=recv,
            device_id=(s if ctx is None else ctx, to), device_id_type=MESH,
        )

    def await_recv(ref, sem):
        remote(ref, ref, sem, sem, me).wait_recv()

    def await_send(ref, sem):
        remote(ref, ref, sem, sem, me).wait_send()

    loads = []
    for k, (src, dst) in enumerate(
        [(tokens_hbm, x_buf.at[me]), (iw_hbm, iw), (gw_hbm, gw), (pw_hbm, pw), (sw_hbm, sw), (cw_hbm, cw), (cb_hbm, cb),
         (sb_hbm, sb), (sg_hbm, sg), (dr_hbm, dr), (cs_hbm, cs), (ow_hbm, ow)]
    ):
        loads.append(pltpu.make_async_copy(src, dst, load_sem.at[k]))
        loads[-1].start()

    barrier = pltpu.get_barrier_semaphore()
    for i in range(1, n_tp):
        pl.semaphore_signal(barrier, inc=1, device_id=(s, lax.rem(me + i, n_tp)), device_id_type=MESH)
    for i in range(1, n_ctx):
        pl.semaphore_signal(barrier, inc=1, device_id=(lax.rem(s + i, n_ctx), me), device_id_type=MESH)
    loads[0].wait()
    pl.semaphore_wait(barrier, n_tp + n_ctx - 2)

    top, bottom = pl.ds(0, half), pl.ds(half, half)
    far_first_x = sorted(range(1, nx), key=lambda d: -min(d, nx - d))
    far_first_y = sorted(range(1, ny), key=lambda d: -min(d, ny - d))
    near_x, near_y = far_first_x[::-1], far_first_y[::-1]

    def send_piece(piece, h, dx, dy, rx, ry):
        view = x_buf.at[piece, bottom if h else top]
        remote(view, view, own_send, own_recv.at[rx * ny + ry, h], tp_at(dx, dy)).start()

    def await_piece(rx, ry, h):
        view = x_buf.at[tp_at(-rx, -ry), bottom if h else top]
        await_recv(view, own_recv.at[rx * ny + ry, h])

    def to_sibling(rx, ry):
        view = x_buf.at[tp_at(-rx, -ry)]
        remote(view, view, sib_send, sib_recv.at[rx * ny + ry], tp_at(0, 0, True)).start()

    def from_sibling(rx, ry):
        await_recv(x_buf.at[tp_at(-rx, -ry, True)], sib_recv.at[rx * ny + ry])

    for k in range(max(nx, ny) - 1):
        if k < nx - 1:
            send_piece(me, 0, far_first_x[k], 0, far_first_x[k], 0)
        if k < ny - 1:
            send_piece(me, 1, 0, far_first_y[k], 0, far_first_y[k])
    to_sibling(0, 0)
    for k in range(max(nx, ny) - 1):
        if k < ny - 1:
            send_piece(me, 0, 0, far_first_y[k], 0, far_first_y[k])
        if k < nx - 1:
            send_piece(me, 1, far_first_x[k], 0, far_first_x[k], 0)

    def times(piece, weight):
        first = pl.multiple_of(piece * width, width)
        return dot(x_buf[piece], weight[pl.ds(first, width), :])

    def add_inner(pieces, fresh=False):
        total = sum(times(p, iw) for p in pieces)
        acc[...] = total if fresh else acc[...] + total

    for load in loads[1:]:
        load.wait()
    decay, carried = dr[...], cs[...]
    from_sibling(0, 0)
    add_inner([tp_at(0, 0), tp_at(0, 0, True)], fresh=True)

    waiting = []
    for k in range(max(nx, ny) - 1):
        group = []
        if k < nx - 1:
            d = near_x[k]
            await_piece(d, 0, 0)
            for e in far_first_y:
                send_piece(tp_at(-d, 0), 0, 0, e, d, e)
            group.append((d, 0))
        if k < ny - 1:
            d = near_y[k]
            await_piece(0, d, 1)
            for e in far_first_x:
                send_piece(tp_at(0, -d), 1, e, 0, e, d)
            group.append((0, d))
        for rx, ry in group:
            await_piece(rx, ry, 1 if ry == 0 else 0)
            to_sibling(rx, ry)
        for rx, ry in waiting:
            from_sibling(rx, ry)
        add_inner([tp_at(-a, -b) for a, b in group] + [tp_at(-a, -b, True) for a, b in waiting])
        waiting = group
    rest = sorted(
        [(a, b) for a in range(1, nx) for b in range(1, ny)],
        key=lambda r: max(near_x.index(r[0]), near_y.index(r[1])) * 10 + near_x.index(r[0]) + near_y.index(r[1]),
    )
    for k in range(0, len(rest), 3):
        group = rest[k : k + 3]
        for rx, ry in group:
            await_piece(rx, ry, 0)
            await_piece(rx, ry, 1)
            to_sibling(rx, ry)
        for rx, ry in waiting:
            from_sibling(rx, ry)
        add_inner([tp_at(-a, -b) for a, b in group] + [tp_at(-a, -b, True) for a, b in waiting])
        waiting = group
    for rx, ry in waiting:
        from_sibling(rx, ry)
    add_inner([tp_at(-a, -b, True) for a, b in waiting])

    pad[8:, :] = acc[...].astype(BF16).astype(F32)
    tail = pad.at[pl.ds(rows, 8)]
    first_shard = s == 0

    @pl.when(s < n_ctx - 1)
    def _():
        remote(tail, tail_in, tail_sem.at[0], tail_sem.at[1], me, ctx=lax.rem(s + 1, n_ctx)).start()

    gate[...] = sum(times(p, gw) for p in range(n_tp)).astype(BF16).astype(F32)

    @pl.when(first_shard)
    def _():
        tail_in[...] = jnp.zeros_like(tail_in)

    @pl.when(s > 0)
    def _():
        await_recv(tail_in, tail_sem.at[1])

    pad[0:8, :] = tail_in[...]
    taps = cw.shape[0]
    summed = cb[...] + cw[0:1, :] * pad[9 - taps : 9 - taps + rows, :]
    for k in range(1, taps):
        summed = summed + cw[k : k + 1, :] * pad[9 - taps + k : 9 - taps + k + rows, :]
    conv_low = silu(summed).astype(BF16)
    conv_ref[...] = conv_low.astype(F32)

    each = p_send.shape[1]
    proj = dot_t(conv_low, pw[:DT_RANK, :]).astype(BF16)
    across = DT_RANK // 128
    for block in range(n_tp * each):
        r, c = block // across, block % across
        p_send[block // each, block % each] = proj[r * 16 : r * 16 + 16, c * 128 : c * 128 + 128]
    bc = dot_t(pw[DT_RANK:, :], conv_low).astype(BF16)
    p_more[0, me] = bc[:STATE]
    p_more[1, me] = bc[STATE:]
    owners = (0, n_tp // 2)
    for i in range(1, n_tp):
        to = lax.rem(me + i, n_tp)
        remote(p_send.at[to], p_recv.at[me], red_sem.at[0], red_sem.at[1], to).start()
    for which, owner in enumerate(owners):
        mine_too = p_more.at[which, me]

        @pl.when(me != owner)
        def _():
            remote(mine_too, mine_too, more_sem.at[which, 0], more_sem.at[which, 1], owner).start()

    p_recv[me] = p_send[me]
    await_recv(p_recv.at[pl.ds(0, n_tp - 1)], red_sem.at[1])
    total = p_recv[0].astype(F32)
    for i in range(1, n_tp):
        total = total + p_recv[i].astype(F32)
    p_res[pl.ds(me * each, each)] = total.astype(BF16)
    result = p_res.at[pl.ds(me * each, each)]
    for i in range(1, n_tp):
        remote(result, result, res_sem.at[0], res_sem.at[1], lax.rem(me + i, n_tp)).start()
    blocks = n_tp * each
    for which, owner in enumerate(owners):
        place = p_res.at[pl.ds(blocks + which, 1)]

        @pl.when(me == owner)
        def _():
            await_recv(p_more.at[which, pl.ds(0, n_tp - 1)], more_sem.at[which, 1])
            total = p_more[which, 0].astype(F32)
            for i in range(1, n_tp):
                total = total + p_more[which, i].astype(F32)
            p_res[blocks + which] = total.astype(BF16)
            for i in range(1, n_tp):
                remote(place, place, more_sem.at[which, 2], more_sem.at[which, 3], lax.rem(me + i, n_tp)).start()

    await_recv(p_res.at[pl.ds(0, (n_tp - 1) * each)], res_sem.at[1])
    low = jnp.concatenate(
        [jnp.concatenate([p_res[r * across + c] for c in range(across)], axis=1) for r in range(rows // 16)], axis=0
    )
    step = jax.nn.softplus(dot(low, sw[...]) + sb[...])
    step_ref[...] = step
    drive_ref[...] = step * conv_ref[...]
    later = lax.broadcasted_iota(jnp.int32, (rows, rows), 0)
    earlier = lax.broadcasted_iota(jnp.int32, (rows, rows), 1)
    below = (earlier <= later).astype(F32)
    so_far = jnp.dot(below, step, preferred_element_type=F32, precision=lax.Precision.HIGHEST)

    for which, owner in enumerate(owners):

        @pl.when(me != owner)
        def _():
            await_recv(p_res.at[pl.ds(blocks + which, 1)], more_sem.at[which, 3])

    b_t, c_t = p_res[blocks].astype(F32), p_res[blocks + 1].astype(F32)
    run = 16
    for k in range(rows // run):
        turn = (rows - k * run) % rows
        b_chunk[k] = pltpu.roll(b_t, turn, 1) if turn else b_t
        c_chunk[k] = pltpu.roll(c_t, turn, 1) if turn else c_t

    def scan_chunk(k, h):
        first = pl.multiple_of(k * run, run)
        steps, drives, bs = step_ref[pl.ds(first, run), :], drive_ref[pl.ds(first, run), :], b_chunk[k]
        for i in range(run):
            h = jnp.exp(-steps[i : i + 1, :] * decay) * h + drives[i : i + 1, :] * bs[:, i : i + 1]
            h_buf[first + i] = h
        return h

    end = lax.fori_loop(0, rows // run, scan_chunk, jnp.zeros((STATE, width), F32))

    state_out[0:STATE, :] = end
    state_out[STATE:, :] = jnp.broadcast_to(so_far[rows - 1 :, :], (8, width))
    for d in range(1, n_ctx):

        @pl.when(s + d < n_ctx)
        def _():
            remote(
                state_out, state_in.at[n_ctx - 1 - d], state_send.at[d], state_recv.at[d], me, ctx=lax.rem(s + d, n_ctx)
            ).start()

    def read_chunk(k, carry):
        first = pl.multiple_of(k * run, run)
        c_now = c_chunk[k]
        lines = []
        for i in range(run):
            lines.append(jnp.sum(h_buf[first + i] * c_now[:, i : i + 1], axis=0, keepdims=True))
        y_buf[pl.ds(first, run), :] = jnp.concatenate(lines, axis=0)
        return carry

    lax.fori_loop(0, rows // run, read_chunk, 0)
    c_rows = jnp.transpose(c_t)
    for n in range(STATE):
        q_buf[n] = c_rows[:, n : n + 1] * jnp.exp(-so_far * decay[n : n + 1, :])
    y_buf[...] = y_buf[...] + sg[...] * conv_ref[...]
    gate[...] = silu(gate[...])

    for d in range(1, n_ctx):

        @pl.when(s >= d)
        def _():
            await_recv(state_in.at[n_ctx - 1 - d], state_recv.at[d])

    def enter(i, e):
        got = state_in[i]
        return jnp.exp(-decay * got[STATE : STATE + 1, :]) * e + got[:STATE, :]

    entering = lax.fori_loop(n_ctx - 1 - s, n_ctx - 1, enter, carried)
    boundary[...] = jnp.exp(-decay * state_out[STATE : STATE + 1, :]) * entering + end

    readout = y_buf[...]
    for n in range(STATE):
        readout = readout + q_buf[n] * entering[n : n + 1, :]
    gated = (readout * gate[...]).astype(BF16)

    def out_piece(piece):
        first = pl.multiple_of(piece * width, width)
        return dot(gated, ow[:, pl.ds(first, width)])

    def combine(ex, ey):
        r = ex * ny + ey
        await_recv(sib_part.at[r], rs_sib_recv.at[r])
        total = mine[r] + sib_part[r].astype(F32)
        mine[r] = total
        s1_send[r] = total.astype(BF16)
        if ey:
            remote(s1_send.at[r, top], s1_a.at[ey, ex], s1_send_sem, s1_a_sem.at[ey, ex], tp_at(0, ey)).start()
        if ex:
            remote(s1_send.at[r, bottom], s1_b.at[ex, ey], s1_send_sem, s1_b_sem.at[ex, ey], tp_at(ex, 0)).start()

    order = [(a, b) for a in far_first_x for b in far_first_y]
    order += [(0, b) for b in far_first_y] + [(a, 0) for a in far_first_x] + [(0, 0)]
    lag = 2
    for k, (ex, ey) in enumerate(order):
        r = ex * ny + ey
        part[r] = out_piece(tp_at(ex, ey, True)).astype(BF16)
        remote(part.at[r], sib_part.at[r], rs_sib_send, rs_sib_recv.at[r], tp_at(0, 0, True)).start()
        mine[r] = out_piece(tp_at(ex, ey))
        if k >= lag:
            combine(*order[k - lag])
    for k in range(max(0, len(order) - lag), len(order)):
        combine(*order[k])

    def second_a(ex):
        total = mine[ex * ny, top, :]
        for e in range(1, ny):
            await_recv(s1_a.at[e, ex], s1_a_sem.at[e, ex])
            total = total + s1_a[e, ex].astype(F32)
        return total

    def second_b(ey):
        total = mine[ey, bottom, :]
        for e in range(1, nx):
            await_recv(s1_b.at[e, ey], s1_b_sem.at[e, ey])
            total = total + s1_b[e, ey].astype(F32)
        return total

    for k in range(max(nx, ny) - 1):
        if k < nx - 1:
            d = far_first_x[k]
            s2_send[0, d] = second_a(d).astype(BF16)
            remote(s2_send.at[0, d], s2_a.at[d], s2_send_sem.at[0, d], s2_a_sem.at[d], tp_at(d, 0)).start()
        if k < ny - 1:
            d = far_first_y[k]
            s2_send[1, d] = second_b(d).astype(BF16)
            remote(s2_send.at[1, d], s2_b.at[d], s2_send_sem.at[1, d], s2_b_sem.at[d], tp_at(0, d)).start()
    upper, lower = second_a(0), second_b(0)
    for d in near_x:
        await_recv(s2_a.at[d], s2_a_sem.at[d])
        upper = upper + s2_a[d].astype(F32)
    mixed[0:half, :] = upper.astype(BF16)
    for d in near_y:
        await_recv(s2_b.at[d], s2_b_sem.at[d])
        lower = lower + s2_b[d].astype(F32)
    mixed[half:, :] = lower.astype(BF16)

    await_send(x_buf.at[pl.ds(0, chips - 1)], own_send)
    await_send(x_buf.at[pl.ds(0, chips)], sib_send)

    @pl.when(s < n_ctx - 1)
    def _():
        await_send(tail, tail_sem.at[0])

    await_send(p_recv.at[pl.ds(0, n_tp - 1)], red_sem.at[0])
    await_send(p_res.at[pl.ds(0, (n_tp - 1) * each)], res_sem.at[0])
    for which, owner in enumerate(owners):

        @pl.when(me != owner)
        def _():
            await_send(p_more.at[which, 0], more_sem.at[which, 0])

        @pl.when(me == owner)
        def _():
            await_send(p_more.at[which, pl.ds(0, n_tp - 1)], more_sem.at[which, 2])

    for d in range(1, n_ctx):

        @pl.when(s + d < n_ctx)
        def _():
            await_send(state_out, state_send.at[d])

    await_send(sib_part, rs_sib_send)
    for a in range(nx):
        for b in range(ny):
            if b:
                await_send(s1_send.at[0, top], s1_send_sem)
            if a:
                await_send(s1_send.at[0, top], s1_send_sem)
    for d in range(1, nx):
        await_send(s2_send.at[0, d], s2_send_sem.at[0, d])
    for d in range(1, ny):
        await_send(s2_send.at[1, d], s2_send_sem.at[1, d])


def on_device(
    n_ctx, n_tp, tokens, inner_weight, gate_weight, conv_weight, conv_bias, proj_weight, step_weight, step_bias, decay_rate,
    skip_gain, out_weight, carried_state,
):
    rows, width = tokens.shape
    depth = inner_weight.shape[0]
    ny, nx = plane_sides(n_tp)
    chips = ny * nx
    half = rows // 2
    each = (rows // 16) * (DT_RANK // 128) // n_tp
    vmem, dma = pltpu.VMEM, pltpu.SemaphoreType.DMA
    args = (
        tokens, inner_weight, gate_weight, conv_weight, conv_bias[None, :], jnp.transpose(proj_weight), step_weight,
        step_bias[None, :], jnp.transpose(decay_rate), skip_gain[None, :], out_weight, jnp.transpose(carried_state),
    )
    held = (inner_weight, gate_weight, out_weight, args[5], step_weight, conv_weight)
    mixed, boundary = pl.pallas_call(
        functools.partial(kernel, n_ctx, n_tp),
        out_shape=(
            jax.ShapeDtypeStruct((rows, width), BF16),
            jax.ShapeDtypeStruct((STATE, width), F32),
        ),
        in_specs=[pl.BlockSpec(memory_space=pl.ANY)] * len(args),
        out_specs=[pl.BlockSpec(memory_space=pltpu.VMEM)] * 2,
        scratch_shapes=[
            vmem((n_tp, rows, width), BF16),
            *[vmem(a.shape, a.dtype) for a in held],
            *[vmem((1, width), F32)] * 3,
            *[vmem((STATE, width), F32)] * 2,
            *[vmem((rows, width), F32)] * 2,
            vmem((rows + 8, width), F32),
            vmem((8, width), F32),
            vmem((n_tp, each, 16, 128), BF16),
            vmem((n_tp, each, 16, 128), BF16),
            vmem((2, n_tp, STATE, 128), BF16),
            vmem((n_tp * each + 2, 16, 128), BF16),
            *[vmem((rows, width), F32)] * 3,
            vmem((rows, STATE, width), F32),
            *[vmem((rows // 16, STATE, rows), F32)] * 2,
            vmem((STATE + 8, width), F32),
            vmem((n_ctx, STATE + 8, width), F32),
            vmem((STATE, rows, width), F32),
            vmem((rows, width), F32),
            *[vmem((chips, rows, width), BF16)] * 2,
            vmem((chips, rows, width), F32),
            vmem((chips, rows, width), BF16),
            vmem((ny, nx, half, width), BF16),
            vmem((nx, ny, half, width), BF16),
            vmem((2, max(nx, ny), half, width), BF16),
            vmem((nx, half, width), BF16),
            vmem((ny, half, width), BF16),
            dma((len(args),)),
            dma,
            dma((chips, 2)),
            dma,
            dma((chips,)),
            dma((2,)),
            dma((2,)),
            dma((2, 4)),
            dma((2,)),
            dma((n_ctx,)),
            dma((n_ctx,)),
            dma,
            dma((chips,)),
            dma,
            dma((ny, nx)),
            dma((nx, ny)),
            dma((2, max(nx, ny))),
            dma((nx,)),
            dma((ny,)),
        ],
        compiler_params=pltpu.CompilerParams(collective_id=0, has_side_effects=True, vmem_limit_bytes=56 << 20),
        cost_estimate=pl.CostEstimate(
            flops=2 * rows * width * (3 * depth + 544 + 512), bytes_accessed=3 * depth * width * 2, transcendentals=0
        ),
        name="layer",
    )(*args)
    return mixed, jnp.transpose(boundary)[None]


def solution(mesh):
    in_specs = (
        P("ctx", "tp"), P(None, "tp"), P(None, "tp"), P(None, "tp"), P("tp"), P("tp", None), P(None, "tp"), P("tp"),
        P("tp", None), P("tp"), P("tp", None), P("tp", None),
    )
    out_specs = (P("ctx", "tp"), P("ctx", "tp", None))
    body = functools.partial(on_device, mesh.shape["ctx"], mesh.shape["tp"])
    return jax.shard_map(body, mesh=mesh, in_specs=in_specs, out_specs=out_specs, check_vma=False)
```

time: 611 us -> 58 us (0.09)
  the two profiles are of different devices: /device:TPU:64 before, /device:TPU:193 now
where the time goes in v1:
time: 58 us; the launch traced here: 57.8 us
  Pallas kernels  54.3 us (94%)
  local copies, waits for them, and re-layouts  2.8 us (5%)
  between operations  0.64 us (1%)
    pallas_call x1, Pallas kernels, on_device(): pl.pallas_call(functools.partial(kernel, n_ctx, n_tp), out_shape=(jax.Sha...  54.3 us
    unnamed x2, local copies, waits for them, and re-layouts  2.8 us

profile of v1, /device:TPU:193, one launch (start us, length us, event | category | flops | bytes accessed | tf_op | source)
XLA Modules:
  0.0 57.8 jit_solution(10195817642979059252)
XLA Ops:
  0.6 54.3 %layer.1 = (bf16[128,256]{1,0:T(8,128)(2,1)}, f32[16,256]{1,0:T(8,128)}) custom-call(bf16[128,256]{1,0:T(8,128)(2,1)} %tokens_hbm.1, bf16[8192,256]{1,0:T(8,128)(2,1)} %iw_hbm.1, bf16[8192,256]{1,0:T(8,128)(2,1)} %gw_hbm.1, f32[4,256]{1,0:T(4,128)} %cw_hbm.1, f32[1,256]{1,0:T(1,128)} %bitcast.13, bf16[544,256]{1,0:T(8,128)(2,1)} %bitcast.9, ...), custom_call_target="tpu_custom_call" | custom-call | flops 1679818752 | bytes 12582912 | tf_op jit(solution)/shard_map/layer/pallas_call | solution.py:437
  55.0 1.5 %copy.16 = bf16[128,256]{1,0:T(8,128)(2,1)} copy(bf16[128,256]{1,0:T(8,128)(2,1)} %get-tuple-element.8) | data formatting | bytes 131072
  56.5 1.3 %copy.17 = f32[1,256,16]{1,2,0:T(8,128)} copy(f32[1,256,16]{1,2,0:T(8,128)} %bitcast.12) | data formatting | bytes 32768

commit v2 on v1

--- a/solution.py
+++ b/solution.py
@@ -40,7 +40,7 @@
     x_buf, iw, gw, ow, pw, sw, cw, cb, sb, sg, dr, cs, acc, gate, pad, tail_in,
     p_send, p_recv, p_more, p_res, step_ref, drive_ref, conv_ref, h_buf, b_chunk, c_chunk, state_out, state_in, q_buf, y_buf,
     part, sib_part, mine, s1_send, s1_a, s1_b, s2_send, s2_a, s2_b,
-    load_sem, own_send, own_recv, sib_send, sib_recv, tail_sem, red_sem, more_sem, res_sem, state_send, state_recv,
+    load_sem, ctx_sem, own_send, own_recv, sib_send, sib_recv, tail_sem, red_sem, more_sem, res_sem, state_send, state_recv,
     rs_sib_send, rs_sib_recv, s1_send_sem, s1_a_sem, s1_b_sem, s2_send_sem, s2_a_sem, s2_b_sem,
 ):
     ny, nx = plane_sides(n_tp)
@@ -78,12 +78,33 @@
         loads[-1].start()
 
     barrier = pltpu.get_barrier_semaphore()
-    for i in range(1, n_tp):
-        pl.semaphore_signal(barrier, inc=1, device_id=(s, lax.rem(me + i, n_tp)), device_id_type=MESH)
-    for i in range(1, n_ctx):
-        pl.semaphore_signal(barrier, inc=1, device_id=(lax.rem(s + i, n_ctx), me), device_id_type=MESH)
+    greeted = [(d, 0) for d in range(1, nx)] + [(0, d) for d in range(1, ny)]
+    for a, b in greeted:
+        pl.semaphore_signal(barrier, inc=1, device_id=(s, tp_at(a, b)), device_id_type=MESH)
+    pl.semaphore_signal(barrier, inc=1, device_id=(s, tp_at(0, 0, True)), device_id_type=MESH)
+    beside = sorted({1, n_ctx - 1}) if n_ctx > 1 else []
+
+    def signal_ctx(sem, by):
+        pl.semaphore_signal(sem, inc=1, device_id=(lax.rem(s + by, n_ctx), me), device_id_type=MESH)
+
+    for by in beside:
+        signal_ctx(barrier, by)
     loads[0].wait()
-    pl.semaphore_wait(barrier, n_tp + n_ctx - 2)
+    pl.semaphore_wait(barrier, len(greeted) + 1 + len(beside))
+    rounds = []
+    reach = 1
+    while 2 * reach < n_ctx:
+        rounds.append(reach)
+        reach *= 2
+
+    def greet_round(i):
+        if i > 0 and i <= len(rounds):
+            pl.semaphore_wait(ctx_sem.at[i - 1], 2)
+        if i < len(rounds):
+            for by in (rounds[i], n_ctx - rounds[i]):
+                signal_ctx(ctx_sem.at[i], by)
+
+    greet_round(0)
 
     top, bottom = pl.ds(0, half), pl.ds(half, half)
     far_first_x = sorted(range(1, nx), key=lambda d: -min(d, nx - d))
@@ -125,6 +146,18 @@
         total = sum(times(p, iw) for p in pieces)
         acc[...] = total if fresh else acc[...] + total
 
+    for k in range(max(nx, ny) - 1):
+        if k < nx - 1:
+            d = near_x[k]
+            await_piece(d, 0, 0)
+            for e in far_first_y:
+                send_piece(tp_at(-d, 0), 0, 0, e, d, e)
+        if k < ny - 1:
+            d = near_y[k]
+            await_piece(0, d, 1)
+            for e in far_first_x:
+                send_piece(tp_at(0, -d), 1, e, 0, e, d)
+    greet_round(1)
     for load in loads[1:]:
         load.wait()
     decay, carried = dr[...], cs[...]
@@ -135,17 +168,9 @@
     for k in range(max(nx, ny) - 1):
         group = []
         if k < nx - 1:
-            d = near_x[k]
-            await_piece(d, 0, 0)
-            for e in far_first_y:
-                send_piece(tp_at(-d, 0), 0, 0, e, d, e)
-            group.append((d, 0))
+            group.append((near_x[k], 0))
         if k < ny - 1:
-            d = near_y[k]
-            await_piece(0, d, 1)
-            for e in far_first_x:
-                send_piece(tp_at(0, -d), 1, e, 0, e, d)
-            group.append((0, d))
+            group.append((0, near_y[k]))
         for rx, ry in group:
             await_piece(rx, ry, 1 if ry == 0 else 0)
             to_sibling(rx, ry)
@@ -171,6 +196,9 @@
         from_sibling(rx, ry)
     add_inner([tp_at(-a, -b, True) for a, b in waiting])
 
+    for i in range(2, len(rounds) + 1):
+        greet_round(i)
+
     pad[8:, :] = acc[...].astype(BF16).astype(F32)
     tail = pad.at[pl.ds(rows, 8)]
     first_shard = s == 0
@@ -207,8 +235,10 @@
     p_more[0, me] = bc[:STATE]
     p_more[1, me] = bc[STATE:]
     owners = (0, n_tp // 2)
-    for i in range(1, n_tp):
-        to = lax.rem(me + i, n_tp)
+    others = [(a, b, o) for a in range(nx) for b in range(ny) for o in (False, True) if a or b or o]
+    others.sort(key=lambda r: -(min(r[0], nx - r[0]) + min(r[1], ny - r[1])))
+    for a, b, other in others:
+        to = tp_at(a, b, other)
         remote(p_send.at[to], p_recv.at[me], red_sem.at[0], red_sem.at[1], to).start()
     for which, owner in enumerate(owners):
         mine_too = p_more.at[which, me]
@@ -224,8 +254,8 @@
         total = total + p_recv[i].astype(F32)
     p_res[pl.ds(me * each, each)] = total.astype(BF16)
     result = p_res.at[pl.ds(me * each, each)]
-    for i in range(1, n_tp):
-        remote(result, result, res_sem.at[0], res_sem.at[1], lax.rem(me + i, n_tp)).start()
+    for a, b, other in others:
+        remote(result, result, res_sem.at[0], res_sem.at[1], tp_at(a, b, other)).start()
     blocks = n_tp * each
     for which, owner in enumerate(owners):
         place = p_res.at[pl.ds(blocks + which, 1)]
@@ -416,6 +446,11 @@
         await_send(s2_send.at[0, d], s2_send_sem.at[0, d])
     for d in range(1, ny):
         await_send(s2_send.at[1, d], s2_send_sem.at[1, d])
+
+
+def hand_on(a_in, b_in, a_out, b_out):
+    a_out[...] = a_in[...]
+    b_out[...] = b_in[...]
 
 
 def on_device(
@@ -470,6 +505,7 @@
             vmem((nx, half, width), BF16),
             vmem((ny, half, width), BF16),
             dma((len(args),)),
+            pltpu.SemaphoreType.REGULAR((4,)),
             dma,
             dma((chips, 2)),
             dma,
@@ -495,6 +531,17 @@
         ),
         name="layer",
     )(*args)
+    mixed, boundary = pl.pallas_call(
+        hand_on,
+        out_shape=(
+            jax.ShapeDtypeStruct((rows, width), BF16),
+            jax.ShapeDtypeStruct((STATE, width), F32),
+        ),
+        in_specs=[pl.BlockSpec(memory_space=pltpu.VMEM)] * 2,
+        out_specs=[pl.BlockSpec(memory_space=pltpu.VMEM)] * 2,
+        cost_estimate=pl.CostEstimate(flops=0, bytes_accessed=4 * rows * width, transcendentals=0),
+        name="results",
+    )(mixed, boundary)
     return mixed, jnp.transpose(boundary)[None]
 
 

time: 58 us -> 52.1 us (0.90)
  the two profiles are of different devices: /device:TPU:193 before, /device:TPU:64 now
where the time goes in v2:
time: 52.1 us; the launch traced here: 51.7 us
  Pallas kernels  51.1 us (98%)
  between operations  0.64 us (1%)
    pallas_call x1, Pallas kernels, on_device(): pl.pallas_call(functools.partial(kernel, n_ctx, n_tp), out_shape=(jax.Sha...  49.6 us
    pallas_call x1, Pallas kernels, on_device(): pl.pallas_call(hand_on, out_shape=(jax.ShapeDtypeStruct((rows, width), BF...  1.48 us

profile of v2, /device:TPU:64, one launch (start us, length us, event | category | flops | bytes accessed | tf_op | source)
XLA Modules:
  0.0 51.7 jit_solution(16260426005159753694)
XLA Ops:
  0.6 49.6 %layer.1 = (bf16[128,256]{1,0:T(8,128)(2,1)}, f32[16,256]{1,0:T(8,128)}) custom-call(bf16[128,256]{1,0:T(8,128)(2,1)} %tokens_hbm.1, bf16[8192,256]{1,0:T(8,128)(2,1)} %iw_hbm.1, bf16[8192,256]{1,0:T(8,128)(2,1)} %gw_hbm.1, f32[4,256]{1,0:T(4,128)} %cw_hbm.1, f32[1,256]{1,0:T(1,128)} %bitcast.12, bf16[544,256]{1,0:T(8,128)(2,1)} %bitcast.9, ...), custom_call_target="tpu_custom_call" | custom-call | flops 1679818752 | bytes 12582912 | tf_op jit(solution)/shard_map/layer/pallas_call | solution.py:472
  50.3 1.5 %results.1 = (bf16[128,256]{1,0:T(8,128)(2,1)}, f32[16,256]{1,0:T(8,128)}) custom-call(bf16[128,256]{1,0:T(8,128)(2,1)} %get-tuple-element.6.a_in, f32[16,256]{1,0:T(8,128)} %get-tuple-element.7.b_in), custom_call_target="tpu_custom_call" | custom-call | bytes 131072 | tf_op jit(solution)/shard_map/results/pallas_call | solution.py:534

commit v3 on v2

--- a/solution.py
+++ b/solution.py
@@ -38,7 +38,7 @@
     n_ctx, n_tp, tokens_hbm, iw_hbm, gw_hbm, cw_hbm, cb_hbm, pw_hbm, sw_hbm, sb_hbm, dr_hbm, sg_hbm, ow_hbm, cs_hbm,
     mixed, boundary,
     x_buf, iw, gw, ow, pw, sw, cw, cb, sb, sg, dr, cs, acc, gate, pad, tail_in,
-    p_send, p_recv, p_more, p_res, step_ref, drive_ref, conv_ref, h_buf, b_chunk, c_chunk, state_out, state_in, q_buf, y_buf,
+    p_send, p_recv, p_more, p_res, step_ref, drive_ref, conv_ref, h_buf, b_chunk, c_chunk, state_out, state_in, sums_out, sums_in, q_buf, y_buf,
     part, sib_part, mine, s1_send, s1_a, s1_b, s2_send, s2_a, s2_b,
     load_sem, ctx_sem, own_send, own_recv, sib_send, sib_recv, tail_sem, red_sem, more_sem, res_sem, state_send, state_recv,
     rs_sib_send, rs_sib_recv, s1_send_sem, s1_a_sem, s1_b_sem, s2_send_sem, s2_a_sem, s2_b_sem,
@@ -69,6 +69,19 @@
     def await_send(ref, sem):
         remote(ref, ref, sem, sem, me).wait_send()
 
+    barrier = pltpu.get_barrier_semaphore()
+    greeted = [(d, 0) for d in range(1, nx)] + [(0, d) for d in range(1, ny)]
+    for a, b in greeted:
+        pl.semaphore_signal(barrier, inc=1, device_id=(s, tp_at(a, b)), device_id_type=MESH)
+    pl.semaphore_signal(barrier, inc=1, device_id=(s, tp_at(0, 0, True)), device_id_type=MESH)
+    beside = sorted({1, n_ctx - 1}) if n_ctx > 1 else []
+
+    def signal_ctx(sem, by):
+        pl.semaphore_signal(sem, inc=1, device_id=(lax.rem(s + by, n_ctx), me), device_id_type=MESH)
+
+    for by in beside:
+        signal_ctx(barrier, by)
+
     loads = []
     for k, (src, dst) in enumerate(
         [(tokens_hbm, x_buf.at[me]), (iw_hbm, iw), (gw_hbm, gw), (pw_hbm, pw), (sw_hbm, sw), (cw_hbm, cw), (cb_hbm, cb),
@@ -77,18 +90,6 @@
         loads.append(pltpu.make_async_copy(src, dst, load_sem.at[k]))
         loads[-1].start()
 
-    barrier = pltpu.get_barrier_semaphore()
-    greeted = [(d, 0) for d in range(1, nx)] + [(0, d) for d in range(1, ny)]
-    for a, b in greeted:
-        pl.semaphore_signal(barrier, inc=1, device_id=(s, tp_at(a, b)), device_id_type=MESH)
-    pl.semaphore_signal(barrier, inc=1, device_id=(s, tp_at(0, 0, True)), device_id_type=MESH)
-    beside = sorted({1, n_ctx - 1}) if n_ctx > 1 else []
-
-    def signal_ctx(sem, by):
-        pl.semaphore_signal(sem, inc=1, device_id=(lax.rem(s + by, n_ctx), me), device_id_type=MESH)
-
-    for by in beside:
-        signal_ctx(barrier, by)
     loads[0].wait()
     pl.semaphore_wait(barrier, len(greeted) + 1 + len(beside))
     rounds = []
@@ -207,6 +208,37 @@
     def _():
         remote(tail, tail_in, tail_sem.at[0], tail_sem.at[1], me, ctx=lax.rem(s + 1, n_ctx)).start()
 
+    taps = cw.shape[0]
+    each = p_send.shape[1]
+    across = DT_RANK // 128
+    early = across // each
+    others = [(a, b, o) for a in range(nx) for b in range(ny) for o in (False, True) if a or b or o]
+    others.sort(key=lambda r: -(min(r[0], nx - r[0]) + min(r[1], ny - r[1])))
+
+    def convolve(first, count):
+        summed = cb[...] + cw[0:1, :] * pad[9 - taps + first : 9 - taps + first + count, :]
+        for k in range(1, taps):
+            summed = summed + cw[k : k + 1, :] * pad[9 - taps + first + k : 9 - taps + first + k + count, :]
+        low_bits = silu(summed).astype(BF16)
+        conv_ref[first : first + count, :] = low_bits.astype(F32)
+        return low_bits
+
+    def project(first, conv_low):
+        proj = dot_t(conv_low, pw[:DT_RANK, :]).astype(BF16)
+        for r in range(first // 16, (first + conv_low.shape[0]) // 16):
+            for c in range(across):
+                block, at = r * across + c, r * 16 - first
+                p_send[block // each, block % each] = proj[at : at + 16, c * 128 : c * 128 + 128]
+
+    def send_block(to):
+        remote(p_send.at[to], p_recv.at[me], red_sem.at[0], red_sem.at[1], to).start()
+
+    conv_rest = convolve(16, rows - 16)
+    project(16, conv_rest)
+    for a, b, other in others:
+        to = tp_at(a, b, other)
+        pl.when(to >= early)(functools.partial(send_block, to))
+
     gate[...] = sum(times(p, gw) for p in range(n_tp)).astype(BF16).astype(F32)
 
     @pl.when(first_shard)
@@ -218,28 +250,15 @@
         await_recv(tail_in, tail_sem.at[1])
 
     pad[0:8, :] = tail_in[...]
-    taps = cw.shape[0]
-    summed = cb[...] + cw[0:1, :] * pad[9 - taps : 9 - taps + rows, :]
-    for k in range(1, taps):
-        summed = summed + cw[k : k + 1, :] * pad[9 - taps + k : 9 - taps + k + rows, :]
-    conv_low = silu(summed).astype(BF16)
-    conv_ref[...] = conv_low.astype(F32)
-
-    each = p_send.shape[1]
-    proj = dot_t(conv_low, pw[:DT_RANK, :]).astype(BF16)
-    across = DT_RANK // 128
-    for block in range(n_tp * each):
-        r, c = block // across, block % across
-        p_send[block // each, block % each] = proj[r * 16 : r * 16 + 16, c * 128 : c * 128 + 128]
-    bc = dot_t(pw[DT_RANK:, :], conv_low).astype(BF16)
+    conv_first = convolve(0, 16)
+    project(0, conv_first)
+    for to in range(early):
+        pl.when(me != to)(functools.partial(send_block, to))
+
+    bc = dot_t(pw[DT_RANK:, :], jnp.concatenate([conv_first, conv_rest], axis=0)).astype(BF16)
     p_more[0, me] = bc[:STATE]
     p_more[1, me] = bc[STATE:]
     owners = (0, n_tp // 2)
-    others = [(a, b, o) for a in range(nx) for b in range(ny) for o in (False, True) if a or b or o]
-    others.sort(key=lambda r: -(min(r[0], nx - r[0]) + min(r[1], ny - r[1])))
-    for a, b, other in others:
-        to = tp_at(a, b, other)
-        remote(p_send.at[to], p_recv.at[me], red_sem.at[0], red_sem.at[1], to).start()
     for which, owner in enumerate(owners):
         mine_too = p_more.at[which, me]
 
@@ -305,15 +324,15 @@
 
     end = lax.fori_loop(0, rows // run, scan_chunk, jnp.zeros((STATE, width), F32))
 
-    state_out[0:STATE, :] = end
-    state_out[STATE:, :] = jnp.broadcast_to(so_far[rows - 1 :, :], (8, width))
-    for d in range(1, n_ctx):
+    state_out[...] = end.astype(BF16)
+    sums_out[...] = so_far[rows - 1 :, :]
+    for d in sorted(range(1, n_ctx), key=lambda d: -min(d, n_ctx - d)):
 
         @pl.when(s + d < n_ctx)
         def _():
-            remote(
-                state_out, state_in.at[n_ctx - 1 - d], state_send.at[d], state_recv.at[d], me, ctx=lax.rem(s + d, n_ctx)
-            ).start()
+            to, slot = lax.rem(s + d, n_ctx), n_ctx - 1 - d
+            remote(state_out, state_in.at[slot], state_send.at[d, 0], state_recv.at[d, 0], me, ctx=to).start()
+            remote(sums_out, sums_in.at[slot], state_send.at[d, 1], state_recv.at[d, 1], me, ctx=to).start()
 
     def read_chunk(k, carry):
         first = pl.multiple_of(k * run, run)
@@ -335,14 +354,14 @@
 
         @pl.when(s >= d)
         def _():
-            await_recv(state_in.at[n_ctx - 1 - d], state_recv.at[d])
+            await_recv(state_in.at[n_ctx - 1 - d], state_recv.at[d, 0])
+            await_recv(sums_in.at[n_ctx - 1 - d], state_recv.at[d, 1])
 
     def enter(i, e):
-        got = state_in[i]
-        return jnp.exp(-decay * got[STATE : STATE + 1, :]) * e + got[:STATE, :]
+        return jnp.exp(-decay * sums_in[i]) * e + state_in[i].astype(F32)
 
     entering = lax.fori_loop(n_ctx - 1 - s, n_ctx - 1, enter, carried)
-    boundary[...] = jnp.exp(-decay * state_out[STATE : STATE + 1, :]) * entering + end
+    boundary[...] = jnp.exp(-decay * sums_out[...]) * entering + end
 
     readout = y_buf[...]
     for n in range(STATE):
@@ -364,7 +383,10 @@
         if ex:
             remote(s1_send.at[r, bottom], s1_b.at[ex, ey], s1_send_sem, s1_b_sem.at[ex, ey], tp_at(ex, 0)).start()
 
-    order = [(a, b) for a in far_first_x for b in far_first_y]
+    order = sorted(
+        [(a, b) for a in far_first_x for b in far_first_y],
+        key=lambda r: (min(far_first_x.index(r[0]), far_first_y.index(r[1])), far_first_x.index(r[0]) + far_first_y.index(r[1])),
+    )
     order += [(0, b) for b in far_first_y] + [(a, 0) for a in far_first_x] + [(0, 0)]
     lag = 2
     for k, (ex, ey) in enumerate(order):
@@ -433,7 +455,8 @@
 
         @pl.when(s + d < n_ctx)
         def _():
-            await_send(state_out, state_send.at[d])
+            await_send(state_out, state_send.at[d, 0])
+            await_send(sums_out, state_send.at[d, 1])
 
     await_send(sib_part, rs_sib_send)
     for a in range(nx):
@@ -492,8 +515,10 @@
             *[vmem((rows, width), F32)] * 3,
             vmem((rows, STATE, width), F32),
             *[vmem((rows // 16, STATE, rows), F32)] * 2,
-            vmem((STATE + 8, width), F32),
-            vmem((n_ctx, STATE + 8, width), F32),
+            vmem((STATE, width), BF16),
+            vmem((n_ctx, STATE, width), BF16),
+            vmem((1, width), F32),
+            vmem((n_ctx, 1, width), F32),
             vmem((STATE, rows, width), F32),
             vmem((rows, width), F32),
             *[vmem((chips, rows, width), BF16)] * 2,
@@ -514,8 +539,8 @@
             dma((2,)),
             dma((2, 4)),
             dma((2,)),
-            dma((n_ctx,)),
-            dma((n_ctx,)),
+            dma((n_ctx, 2)),
+            dma((n_ctx, 2)),
             dma,
             dma((chips,)),
             dma,

time: 52.1 us -> 51 us (0.979)
  Pallas kernels: 51.1 us -> 50.2 us
    pallas_call x1, Pallas kernels: 49.6 us -> 48.8 us  [on_device(): pl.pallas_call(functools.partial(kernel, n_ctx, n_tp), out_shape=(jax.Sha...]
where the time goes in v3:
time: 51 us; the launch traced here: 50.9 us
  Pallas kernels  50.2 us (98%)
  between operations  0.64 us (1%)
    pallas_call x1, Pallas kernels, on_device(): pl.pallas_call(functools.partial(kernel, n_ctx, n_tp), out_shape=(jax.Sha...  48.8 us
    pallas_call x1, Pallas kernels, on_device(): pl.pallas_call(hand_on, out_shape=(jax.ShapeDtypeStruct((rows, width), BF...  1.48 us

profile of v3, /device:TPU:64, one launch (start us, length us, event | category | flops | bytes accessed | tf_op | source)
XLA Modules:
  0.0 50.9 jit_solution(9079935328216813705)
XLA Ops:
  0.6 48.8 %layer.1 = (bf16[128,256]{1,0:T(8,128)(2,1)}, f32[16,256]{1,0:T(8,128)}) custom-call(bf16[128,256]{1,0:T(8,128)(2,1)} %tokens_hbm.1, bf16[8192,256]{1,0:T(8,128)(2,1)} %iw_hbm.1, bf16[8192,256]{1,0:T(8,128)(2,1)} %gw_hbm.1, f32[4,256]{1,0:T(4,128)} %cw_hbm.1, f32[1,256]{1,0:T(1,128)} %bitcast.12, bf16[544,256]{1,0:T(8,128)(2,1)} %bitcast.9, ...), custom_call_target="tpu_custom_call" | custom-call | flops 1679818752 | bytes 12582912 | tf_op jit(solution)/shard_map/layer/pallas_call | solution.py:495
  49.4 1.5 %results.1 = (bf16[128,256]{1,0:T(8,128)(2,1)}, f32[16,256]{1,0:T(8,128)}) custom-call(bf16[128,256]{1,0:T(8,128)(2,1)} %get-tuple-element.6.a_in, f32[16,256]{1,0:T(8,128)} %get-tuple-element.7.b_in), custom_call_target="tpu_custom_call" | custom-call | bytes 131072 | tf_op jit(solution)/shard_map/results/pallas_call | solution.py:559

commit v4 on v3

--- a/solution.py
+++ b/solution.py
@@ -322,7 +322,7 @@
             h_buf[first + i] = h
         return h
 
-    end = lax.fori_loop(0, rows // run, scan_chunk, jnp.zeros((STATE, width), F32))
+    end = lax.fori_loop(0, rows // run, scan_chunk, jnp.zeros((STATE, width), F32), unroll=True)
 
     state_out[...] = end.astype(BF16)
     sums_out[...] = so_far[rows - 1 :, :]

time: 51 us -> 50.5 us (level)
    pallas_call x1, Pallas kernels: 48.8 us -> 48.2 us  [on_device(): pl.pallas_call(functools.partial(kernel, n_ctx, n_tp), out_shape=(jax.Sha...]
where the time goes in v4:
time: 50.5 us; the launch traced here: 50.4 us
  Pallas kernels  49.7 us (98%)
  between operations  0.64 us (1%)
    pallas_call x1, Pallas kernels, on_device(): pl.pallas_call(functools.partial(kernel, n_ctx, n_tp), out_shape=(jax.Sha...  48.2 us
    pallas_call x1, Pallas kernels, on_device(): pl.pallas_call(hand_on, out_shape=(jax.ShapeDtypeStruct((rows, width), BF...  1.48 us

profile of v4, /device:TPU:64, one launch (start us, length us, event | category | flops | bytes accessed | tf_op | source)
XLA Modules:
  0.0 50.4 jit_solution(7674988481781968760)
XLA Ops:
  0.6 48.2 %layer.1 = (bf16[128,256]{1,0:T(8,128)(2,1)}, f32[16,256]{1,0:T(8,128)}) custom-call(bf16[128,256]{1,0:T(8,128)(2,1)} %tokens_hbm.1, bf16[8192,256]{1,0:T(8,128)(2,1)} %iw_hbm.1, bf16[8192,256]{1,0:T(8,128)(2,1)} %gw_hbm.1, f32[4,256]{1,0:T(4,128)} %cw_hbm.1, f32[1,256]{1,0:T(1,128)} %bitcast.12, bf16[544,256]{1,0:T(8,128)(2,1)} %bitcast.9, ...), custom_call_target="tpu_custom_call" | custom-call | flops 1679818752 | bytes 12582912 | tf_op jit(solution)/shard_map/layer/pallas_call | solution.py:495
  48.9 1.5 %results.1 = (bf16[128,256]{1,0:T(8,128)(2,1)}, f32[16,256]{1,0:T(8,128)}) custom-call(bf16[128,256]{1,0:T(8,128)(2,1)} %get-tuple-element.6.a_in, f32[16,256]{1,0:T(8,128)} %get-tuple-element.7.b_in), custom_call_target="tpu_custom_call" | custom-call | bytes 131072 | tf_op jit(solution)/shard_map/results/pallas_call | solution.py:559
